TPU v7x, 32 devices: a whole 2x2x4 slice. The times are simulated.
32 devices in a mesh: clip: 2 (over x), gz: 16 (over z, y, core).
Axes of the slice: x: 2, y: 2, z: 4, core: 2. Of those that a mesh axis runs over, the one named last changes fastest.
Arguments:
- source_term: float32 [2, 128, 64, 128], P(None, ('clip', 'gz')), parts along dimension 1, may hold values from -24 to 24
- material: int32 [128, 64, 128], P(('clip', 'gz')), parts along dimension 0, may hold values from 0 to 2
- orders: int32 [2, 1024], P(None, 'gz'), may hold values from -22 to 22
Outputs:
- solution: float32 [2, 128, 64, 128], P(None, ('clip', 'gz')), parts along dimension 1
- residual: float32 [2, 128, 64, 128], P(None, ('clip', 'gz')), parts along dimension 1
- pupil_orders: float32 [2, 2048], P(None, ('clip', 'gz')), parts along dimension 1
There are 2 independent parts, one for each index of `clip`. A program takes and returns all parts, laid end to end along the dimension named above; an argument that names none is the same for every part. Nothing has to cross between parts.
All inputs are finite; a program needn't handle non-finite values.
Results may differ from a plain program's by a relative error of at most 0.0003.
Values sent between devices are 32-bit elements; how exact they have to be, the bound alone decides.
A program may use at most 128 MiB of HBM per device.

v0:
```python
import functools
import math

import jax
import jax.numpy as jnp
import numpy as np
from jax import lax
from jax.experimental import pallas as pl
from jax.experimental.pallas import tpu as pltpu
from jax.sharding import PartitionSpec as P

ORD_HALF = 22
HELM_TABLE = ((-0.5, 0.0), (1.0, -1.4), (-1.2, 0.0))
SHIFT_TABLE = ((-0.5, -0.25), (1.0, -0.25 * math.sqrt(11.84)), (-1.2, -0.6))
RELAX = 0.8
REACH1 = 3
REACH2 = 5
HALF = 64
HARM = 48
F32 = jnp.float32


def weight_of(shift):
    bottom = complex(6.0 + shift[0], shift[1])
    value = RELAX / bottom
    return (value.real, value.imag)


WEIGHT_TABLE = tuple(weight_of(entry) for entry in SHIFT_TABLE)
DIAG_TABLE = tuple((6.0 + entry[0], entry[1]) for entry in SHIFT_TABLE)
IMAGE_TABLE = tuple((6.0 + entry[0], entry[1]) for entry in HELM_TABLE)


def pick(material, table):
    one = material == 1
    two = material == 2
    return tuple(
        jnp.where(one, table[1][k], jnp.where(two, table[2][k], table[0][k])).astype(F32)
        for k in range(2)
    )


def mul(ar, ai, br, bi):
    return ar * br - ai * bi, ar * bi + ai * br


def loop(lo, hi, body):
    def step(p, carry):
        body(p)
        return carry

    lax.fori_loop(lo, hi, step, 0)


def around(ref, k, p, lane_step):
    x = ref[k, p]
    rows = x.shape[0]
    lanes = x.shape[1]
    total = ref[k, p - 1] + ref[k, p + 1]
    total = total + (pltpu.roll(x, 1, 0) + pltpu.roll(x, rows - 1, 0))
    return total + (pltpu.roll(x, lane_step, 1) + pltpu.roll(x, lanes - lane_step, 1))


def first_sweep(dst, rhs, weight, p):
    r, i = mul(weight[0, p], weight[1, p], rhs[0, p], rhs[1, p])
    dst[0, p] = r
    dst[1, p] = i


def sweep(dst, old, rhs, weight, p, lane_step, h2):
    nr = around(old, 0, p, lane_step)
    ni = around(old, 1, p, lane_step)
    if h2 != 1.0:
        nr, ni = nr * h2, ni * h2
    r, i = mul(weight[0, p], weight[1, p], rhs[0, p] + nr, rhs[1, p] + ni)
    dst[0, p] = (1.0 - RELAX) * old[0, p] + r
    dst[1, p] = (1.0 - RELAX) * old[1, p] + i


def lane_iota(shape):
    return lax.broadcasted_iota(jnp.int32, shape, 1)


def pair_lanes(x, step):
    lanes = x.shape[1]
    low = (lane_iota(x.shape) & step) == 0
    return x + jnp.where(low, pltpu.roll(x, lanes - step, 1), pltpu.roll(x, step, 1))


def pair_rows(x, tmp):
    rows = x.shape[0]
    tmp[0:rows] = x
    return tmp[pl.ds(0, rows // 2, stride=2)] + tmp[pl.ds(1, rows // 2, stride=2)]


def spread_rows(x, tmp):
    rows = x.shape[0]
    tmp[pl.ds(0, rows, stride=2)] = x
    tmp[pl.ds(1, rows, stride=2)] = x
    return tmp[0 : 2 * rows]


def pack_two(r, i):
    return jnp.where((lane_iota(r.shape) & 1) == 0, r, i)


def unpack_two(x):
    lanes = x.shape[1]
    even = (lane_iota(x.shape) & 1) == 0
    return jnp.where(even, x, pltpu.roll(x, 1, 1)), jnp.where(even, pltpu.roll(x, lanes - 1, 1), x)


def pack_four(r, i):
    rows = r.shape[0] // 2
    top = pack_two(r[:rows], i[:rows])
    low = pack_two(r[rows:], i[rows:])
    return jnp.where((lane_iota(top.shape) & 2) == 0, top, low)


def unpack_four(x):
    lanes = x.shape[1]
    first = (lane_iota(x.shape) & 2) == 0
    halves = []
    for y in unpack_two(x):
        halves.append(
            (jnp.where(first, y, pltpu.roll(y, 2, 1)), jnp.where(first, pltpu.roll(y, lanes - 2, 1), y))
        )
    return halves


def invert(r, i):
    bottom = 1.0 / (r * r + i * i)
    return RELAX * r * bottom, -RELAX * i * bottom


def precise(a, b, dims):
    return lax.dot_general(
        a, b, (dims, ((), ())), precision=lax.Precision.HIGHEST, preferred_element_type=F32
    )


def spectrum_of(r, i, ty, tx):
    gr = precise(ty, r, ((1,), (1,)))
    gi = precise(ty, i, ((1,), (1,)))
    inner = jnp.concatenate([gr[:HALF] - gi[HALF:], gr[HALF:] + gi[:HALF]], axis=0)
    outer = precise(inner, tx, ((1,), (0,)))
    turned = pltpu.roll(outer[HALF:], HALF, 1)
    left = lane_iota(turned.shape) < HALF
    return (outer[:HALF] + jnp.where(left, -turned, turned))[:HARM]


def tables(nx, ny):
    harmonics = np.arange(2 * ORD_HALF + 1) - ORD_HALF
    count = harmonics.size
    ty = np.zeros((2 * HALF, ny), np.float32)
    angle = 2.0 * np.pi * ((harmonics[:, None] * np.arange(ny)[None, :]) % ny) / ny
    ty[:count] = np.cos(angle)
    ty[HALF : HALF + count] = -np.sin(angle)
    tx = np.zeros((nx, 2 * HALF), np.float32)
    angle = 2.0 * np.pi * ((np.arange(nx)[:, None] * harmonics[None, :]) % nx) / nx
    scale = 1.0 / math.sqrt(nx * ny)
    tx[:, :count] = np.cos(angle) * scale
    tx[:, HALF : HALF + count] = -np.sin(angle) * scale
    return ty, tx


def kernel(
    n, src, mat, ords, ty, tx, sol, res, pup,
    fx, gx, mx, w0, va, vb, d1, w1, f1, v1a, v1b, w2, f2, v2a, v2b, d2,
    pk1, pk2, tmp, red, spec,
    fine_send, fine_recv, k1_send, k1_recv, k2_send, k2_recv,
    red_send, red_recv, spec_send, spec_recv,
):
    me = lax.axis_index("gz")
    own = src.shape[1]
    depth = own
    half = own // 2
    mid1 = REACH1 * half
    sent = []

    def other(k):
        return {"gz": lax.rem(me + k + n, n)}

    def start(source, target, ssem, rsem, k):
        copy = pltpu.make_async_remote_copy(
            src_ref=source, dst_ref=target, send_sem=ssem, recv_sem=rsem,
            device_id=other(k), device_id_type=pl.DeviceIdType.MESH,
        )
        copy.start()
        sent.append(copy)
        return copy

    barrier = pltpu.get_barrier_semaphore()

    def greet(k):
        pl.semaphore_signal(
            barrier, inc=1, device_id={"gz": lax.rem(me + k, n)},
            device_id_type=pl.DeviceIdType.MESH,
        )

    loop(1, n, greet)

    def take(p):
        m = mat[p]
        mx[depth + p] = m
        fx[0, depth + p] = src[0, p]
        fx[1, depth + p] = src[1, p]

    loop(0, own, take)

    for p in range(half):
        a = pick(mat[2 * p], SHIFT_TABLE)
        b = pick(mat[2 * p + 1], SHIFT_TABLE)
        for k in range(2):
            d1[k, p] = 0.125 * pair_rows(pair_lanes(a[k] + b[k], 1), tmp)
        pk1[0, REACH1, p] = pack_two(d1[0, p], d1[1, p])
    for k in range(2):
        d2[k] = 0.125 * pair_rows(pair_lanes(d1[k, 0] + d1[k, 1], 2), tmp)
    pk2[0, REACH2] = pack_four(d2[0], d2[1])

    pl.semaphore_wait(barrier, n - 1)

    def send_planes(source, base, target, slot, near, dims):
        up_from = half if near else 0
        up_to = half if near else 0
        down_from = 0 if near else half
        down_to = depth + own + (0 if near else half)
        copies = []
        for which, (k, a, b) in enumerate(((1, up_from, up_to), (-1, down_from, down_to))):
            s = pl.ds(base + a, half)
            t = pl.ds(b, half)
            one = source.at[:, s] if dims else source.at[s]
            two = target.at[:, t] if dims else target.at[t]
            copies.append(
                start(one, two, fine_send.at[slot + which], fine_recv.at[slot + which], k)
            )
        return copies

    def send_one(which):
        copies = {}
        for k in range(1, REACH1 + 1):
            for d in (k, -k):
                at = which * (2 * REACH1 + 1) + REACH1 - d
                copies[-d] = start(
                    pk1.at[which, REACH1], pk1.at[which, REACH1 - d],
                    k1_send.at[at], k1_recv.at[at], d,
                )
        return copies

    def send_two(which):
        copies = {}
        for k in range(1, REACH2 + 1):
            for d in (k, -k):
                at = which * (2 * REACH2 + 1) + REACH2 - d
                copies[-d] = start(
                    pk2.at[which, REACH2], pk2.at[which, REACH2 - d],
                    k2_send.at[at], k2_recv.at[at], d,
                )
        return copies

    near_mat = send_planes(mat, 0, mx, 0, True, False)
    near_src = send_planes(src, 0, fx, 2, True, True)
    shifts1 = send_one(0)
    shifts2 = send_two(0)
    far_mat = send_planes(mat, 0, mx, 4, False, False)
    far_src = send_planes(src, 0, fx, 6, False, True)

    def inside(plane, count):
        return jnp.where(jnp.logical_and(plane >= 0, plane < count), 1.0, 0.0).astype(F32)

    def weight0(p):
        m = inside(me * own + p - depth, n * own)
        r, i = pick(mx[p], WEIGHT_TABLE)
        w0[0, p] = r * m
        w0[1, p] = i * m

    def weight1(p):
        r, i = unpack_two(pk1[0, p // half, p % half])
        r, i = invert(r + 1.5, i)
        m = inside(me * half + p - mid1, n * half)
        w1[0, p] = r * m
        w1[1, p] = i * m

    def weight2(p):
        (rt, rb), (it, ib) = unpack_four(pk2[0, p])
        rows = rt.shape[0]
        m = inside(me + p - REACH2, n)
        for at, (r, i) in enumerate(((rt, it), (rb, ib))):
            r, i = invert(r + 0.375, i)
            w2[0, p, at * rows : (at + 1) * rows] = r * m
            w2[1, p, at * rows : (at + 1) * rows] = i * m

    def take1(which):
        def body(p):
            r, i = unpack_two(pk1[which, p // half, p % half])
            f1[0, p] = r
            f1[1, p] = i

        return body

    def take2(which):
        def body(p):
            (rt, rb), (it, ib) = unpack_four(pk2[which, p])
            rows = rt.shape[0]
            f2[0, p, 0:rows] = rt
            f2[0, p, rows : 2 * rows] = rb
            f2[1, p, 0:rows] = it
            f2[1, p, rows : 2 * rows] = ib

        return body

    def cycle(which, f, near, far):
        begin, end = depth, depth + own
        if which == 1:
            for copy in near_mat:
                copy.wait_recv()
            loop(begin - 2, end + 2, weight0)
        for copy in near:
            copy.wait_recv()
        loop(begin - 2, end + 2, lambda p: first_sweep(va, f, w0, p))
        loop(begin - 1, end + 1, lambda p: sweep(vb, va, f, w0, p, 1, 1.0))

        def down(q):
            total = [None, None]
            for s in range(2):
                p = depth + 2 * q + s
                c = pick(mx[p], DIAG_TABLE)
                dr, di = mul(c[0], c[1], vb[0, p], vb[1, p])
                for k, d in enumerate((dr, di)):
                    e = (f[k, p] - d) + around(vb, k, p, 1)
                    total[k] = e if s == 0 else total[k] + e
            parts = [0.125 * pair_rows(pair_lanes(t, 1), tmp) for t in total]
            f1[0, mid1 + q] = parts[0]
            f1[1, mid1 + q] = parts[1]
            pk1[which, REACH1, q] = pack_two(parts[0], parts[1])

        for q in range(half):
            down(q)
        ones = send_one(which)

        if which == 1:
            for d in (-1, 1):
                shifts1[d].wait_recv()
            loop(mid1 - half, mid1 + 2 * half, weight1)

        for d in (-1, 1):
            ones[d].wait_recv()
        loop(mid1 - half, mid1, take1(which))
        loop(mid1 + half, mid1 + 2 * half, take1(which))
        loop(mid1 - 2, mid1 + half + 2, lambda p: first_sweep(v1a, f1, w1, p))
        loop(mid1 - 1, mid1 + half + 1, lambda p: sweep(v1b, v1a, f1, w1, p, 2, 0.25))

        parts = []
        total = [None, None]
        for q in range(half):
            p = mid1 + q
            dr, di = mul(d1[0, q] + 1.5, d1[1, q], v1b[0, p], v1b[1, p])
            for k, d in enumerate((dr, di)):
                e = (f1[k, p] - d) + 0.25 * around(v1b, k, p, 2)
                total[k] = e if q == 0 else total[k] + e
        parts = [0.125 * pair_rows(pair_lanes(t, 2), tmp) for t in total]
        pk2[which, REACH2] = pack_four(parts[0], parts[1])
        twos = send_two(which)

        if which == 1:
            for copy in far_mat:
                copy.wait_recv()
            loop(0, begin - 2, weight0)
            loop(end + 2, end + depth, weight0)
            for d in range(2, REACH1 + 1):
                shifts1[d].wait_recv()
                shifts1[-d].wait_recv()
            loop(1, mid1 - half, weight1)
            loop(mid1 + 2 * half, 2 * mid1 + half - 1, weight1)
        for d in range(2, REACH1 + 1):
            ones[d].wait_recv()
            ones[-d].wait_recv()
        loop(1, mid1 - half, take1(which))
        loop(mid1 + 2 * half, 2 * mid1 + half - 1, take1(which))
        loop(1, mid1 - 2, lambda p: first_sweep(v1a, f1, w1, p))
        loop(mid1 + half + 2, 2 * mid1 + half - 1, lambda p: first_sweep(v1a, f1, w1, p))
        loop(2, mid1 - 1, lambda p: sweep(v1b, v1a, f1, w1, p, 2, 0.25))
        loop(mid1 + half + 1, 2 * mid1 + half - 2, lambda p: sweep(v1b, v1a, f1, w1, p, 2, 0.25))
        for copy in far:
            copy.wait_recv()
        loop(0, begin - 2, lambda p: first_sweep(va, f, w0, p))
        loop(end + 2, end + depth, lambda p: first_sweep(va, f, w0, p))
        loop(1, begin - 1, lambda p: sweep(vb, va, f, w0, p, 1, 1.0))
        loop(end + 1, end + depth - 1, lambda p: sweep(vb, va, f, w0, p, 1, 1.0))
        if which == 1:
            for d in range(1, REACH2 + 1):
                shifts2[d].wait_recv()
                shifts2[-d].wait_recv()
            loop(0, 2 * REACH2 + 1, weight2)

        for d in range(1, REACH2 + 1):
            twos[d].wait_recv()
            twos[-d].wait_recv()
        loop(0, 2 * REACH2 + 1, take2(which))
        loop(0, 2 * REACH2 + 1, lambda p: first_sweep(v2a, f2, w2, p))
        loop(1, 2 * REACH2, lambda p: sweep(v2b, v2a, f2, w2, p, 4, 0.0625))
        loop(2, 2 * REACH2 - 1, lambda p: sweep(v2a, v2b, f2, w2, p, 4, 0.0625))
        loop(3, 2 * REACH2 - 2, lambda p: sweep(v2b, v2a, f2, w2, p, 4, 0.0625))

        def raise1(c):
            p = (c - REACH2 + REACH1) * half
            for k in range(2):
                x = spread_rows(v2b[k, c], tmp)
                v1b[k, p] = v1b[k, p] + x
                v1b[k, p + 1] = v1b[k, p + 1] + x

        loop(REACH2 - 2, REACH2 + 3, raise1)
        loop(mid1 - 3, mid1 + half + 3, lambda p: sweep(v1a, v1b, f1, w1, p, 2, 0.25))
        loop(mid1 - 2, mid1 + half + 2, lambda p: sweep(v1b, v1a, f1, w1, p, 2, 0.25))

        def raise0(c):
            p = depth + 2 * (c - mid1)
            for k in range(2):
                x = spread_rows(v1b[k, c], tmp)
                vb[k, p] = vb[k, p] + x
                vb[k, p + 1] = vb[k, p + 1] + x

        loop(mid1 - 2, mid1 + half + 2, raise0)
        loop(begin - 2, end + 2, lambda p: sweep(va, vb, f, w0, p, 1, 1.0))
        loop(begin - 1, end + 1, lambda p: sweep(vb, va, f, w0, p, 1, 1.0))

    def image_of(p):
        c = pick(mx[p], IMAGE_TABLE)
        r, i = mul(c[0], c[1], vb[0, p], vb[1, p])
        return r - around(vb, 0, p, 1), i - around(vb, 1, p, 1)

    def fold(x):
        rows, lanes = x.shape
        return jnp.sum(x.reshape(rows // 8, 8, lanes), axis=0)

    def share(which, sums):
        rows = [jnp.sum(s, axis=0, keepdims=True) for s in sums]
        rows.append(jnp.zeros((8 - len(rows), rows[0].shape[1]), F32))
        red[which, me] = jnp.concatenate(rows, axis=0)

        def post(k):
            pltpu.make_async_remote_copy(
                src_ref=red.at[which, me], dst_ref=red.at[which, me],
                send_sem=red_send.at[which, k], recv_sem=red_recv.at[which, k],
                device_id={"gz": lax.rem(me + k, n)}, device_id_type=pl.DeviceIdType.MESH,
            ).start()

        loop(1, n, post)

    def collect(which):
        def await_one(k):
            one = pltpu.make_async_remote_copy(
                src_ref=red.at[which, me], dst_ref=red.at[which, lax.rem(me + n - k, n)],
                send_sem=red_send.at[which, k], recv_sem=red_recv.at[which, k],
                device_id={"gz": lax.rem(me + k, n)}, device_id_type=pl.DeviceIdType.MESH,
            )
            one.wait_recv()
            one.wait_send()

        loop(1, n, await_one)
        total = red[which, 0]
        for j in range(1, n):
            total = total + red[which, j]
        total = jnp.sum(total, axis=1, keepdims=True)
        return total[0:1], total[1:2], total[2:3]

    def spectrum(which):
        def post(k):
            pltpu.make_async_remote_copy(
                src_ref=spec.at[which], dst_ref=spec.at[which],
                send_sem=spec_send.at[which, k], recv_sem=spec_recv.at[which],
                device_id={"gz": lax.rem(me + k, n)}, device_id_type=pl.DeviceIdType.MESH,
            ).start()

        @pl.when(me == n - 1)
        def _():
            last = depth + own - 1
            spec[which] = spectrum_of(vb[0, last], vb[1, last], ty[...], tx[...])
            loop(1, n, post)

    def orders_of(which):
        def settle(k):
            pltpu.make_async_remote_copy(
                src_ref=spec.at[which], dst_ref=spec.at[which],
                send_sem=spec_send.at[which, k], recv_sem=spec_recv.at[which],
                device_id={"gz": lax.rem(me + k, n)}, device_id_type=pl.DeviceIdType.MESH,
            ).wait_send()

        @pl.when(me == n - 1)
        def _():
            loop(1, n, settle)

        @pl.when(me != n - 1)
        def _():
            pltpu.make_async_remote_copy(
                src_ref=spec.at[which], dst_ref=spec.at[which],
                send_sem=spec_send.at[which, 0], recv_sem=spec_recv.at[which],
                device_id={"gz": lax.rem(me + 1, n)}, device_id_type=pl.DeviceIdType.MESH,
            ).wait_recv()

        count = ords.shape[1]
        x = ords[0:1] + ORD_HALF
        y = ords[1:2] + ORD_HALF
        row = lax.broadcasted_iota(jnp.int32, (2 * HALF, count), 0)
        pick_y = lax.broadcasted_iota(jnp.int32, (HARM, count), 0) == y
        out = []
        for k in range(2):
            pick_x = jnp.where(row == x + k * HALF, 1.0, 0.0).astype(F32)
            chosen = precise(spec[which], pick_x, ((1,), (0,)))
            out.append(jnp.sum(jnp.where(pick_y, chosen, 0.0), axis=0, keepdims=True))
        return out

    cycle(1, fx, near_src, far_src)

    zero = jnp.zeros((8, src.shape[3]), F32)
    sums = [zero, zero, zero]
    for p in range(own):
        r, i = image_of(depth + p)
        gx[0, depth + p] = r
        gx[1, depth + p] = i
        a, b = src[0, p], src[1, p]
        sums[0] = sums[0] + fold(a * a + b * b)
        sums[1] = sums[1] + fold(a * r + b * i)
        sums[2] = sums[2] + fold(a * i - b * r)
    near_img = send_planes(gx, depth, gx, 8, True, True)
    share(0, sums)
    far_img = send_planes(gx, depth, gx, 10, False, True)

    def keep(p):
        sol[0, p] = vb[0, depth + p]
        sol[1, p] = vb[1, depth + p]

    loop(0, own, keep)
    spectrum(0)

    cycle(2, gx, near_img, far_img)

    rho, cr, ci = collect(0)
    scale = rho / (cr * cr + ci * ci)
    ar, ai = cr * scale, -(ci * scale)

    sums = [zero, zero, zero]
    for p in range(own):
        e = depth + p
        r, i = image_of(e)
        gr, gi = gx[0, e], gx[1, e]
        tr, ti = mul(ar, ai, gr, gi)
        hr, hi = src[0, p] - tr, src[1, p] - ti
        tr, ti = mul(ar, ai, r, i)
        lr, li = gr - tr, gi - ti
        va[0, e], va[1, e] = lr, li
        res[0, p], res[1, p] = hr, hi
        sums[0] = sums[0] + fold(lr * hr + li * hi)
        sums[1] = sums[1] + fold(lr * hi - li * hr)
        sums[2] = sums[2] + fold(lr * lr + li * li)
    share(1, sums)
    spectrum(1)
    sdr, sdi = orders_of(0)

    along_r, along_i, norm = collect(1)
    wr, wi = along_r / norm, along_i / norm

    def finish(p):
        e = depth + p
        dr, di = sol[0, p], sol[1, p]
        tr, ti = mul(ar, ai, vb[0, e], vb[1, e])
        cr_, ci_ = mul(wr, wi, dr - tr, di - ti)
        xr, xi = mul(ar, ai, dr, di)
        sol[0, p], sol[1, p] = xr + cr_, xi + ci_
        tr, ti = mul(wr, wi, va[0, e], va[1, e])
        res[0, p], res[1, p] = res[0, p] - tr, res[1, p] - ti

    loop(0, own, finish)

    sqr, sqi = orders_of(1)
    tr, ti = mul(ar, ai, sqr, sqi)
    cr_, ci_ = mul(wr, wi, sdr - tr, sdi - ti)
    xr, xi = mul(ar, ai, sdr, sdi)
    pup[0:1] = xr + cr_
    pup[1:2] = xi + ci_

    for copy in sent:
        copy.wait_send()


def on_device(n, source_term, material, orders):
    own, nx, ny = material.shape
    half = own // 2
    ty, tx = tables(nx, ny)
    vm = pltpu.VMEM
    fine = vm((2, 3 * own, nx, ny), F32)
    planes1 = (2 * REACH1 + 1) * half
    one = vm((2, planes1, nx // 2, ny), F32)
    planes2 = 2 * REACH2 + 1
    two = vm((2, planes2, nx // 4, ny), F32)
    dma = pltpu.SemaphoreType.DMA
    ext1 = 3 * (2 * REACH1 + 1)
    ext2 = 3 * planes2
    whole = pl.BlockSpec(memory_space=pltpu.VMEM)
    return pl.pallas_call(
        functools.partial(kernel, n),
        out_shape=(
            jax.ShapeDtypeStruct(source_term.shape, F32),
            jax.ShapeDtypeStruct(source_term.shape, F32),
            jax.ShapeDtypeStruct(orders.shape, F32),
        ),
        in_specs=[whole] * 5,
        out_specs=(whole,) * 3,
        scratch_shapes=[
            fine, fine, vm((3 * own, nx, ny), jnp.int32), fine, fine, fine,
            vm((2, half, nx // 2, ny), F32), one, one, one, one,
            two, two, two, two, vm((2, nx // 4, ny), F32),
            vm((3, 2 * REACH1 + 1, half, nx // 2, ny), F32),
            vm((3, planes2, nx // 8, ny), F32),
            vm((nx, ny), F32),
            vm((2, n, 8, ny), F32),
            vm((2, HARM, 2 * HALF), F32),
            dma((12,)), dma((12,)), dma((ext1,)), dma((ext1,)), dma((ext2,)), dma((ext2,)),
            dma((2, n)), dma((2, n)), dma((2, n)), dma((2,)),
        ],
        compiler_params=pltpu.CompilerParams(
            collective_id=0, has_side_effects=True, vmem_limit_bytes=40 * 1024 * 1024
        ),
    )(source_term, material, orders, jnp.asarray(ty), jnp.asarray(tx))


def solution(mesh):
    return jax.shard_map(
        functools.partial(on_device, mesh.shape["gz"]),
        mesh=mesh,
        in_specs=(
            P(None, ("clip", "gz"), None, None),
            P(("clip", "gz"), None, None),
            P(None, "gz"),
        ),
        out_specs=(
            P(None, ("clip", "gz"), None, None),
            P(None, ("clip", "gz"), None, None),
            P(None, ("clip", "gz")),
        ),
        check_vma=False,
    )
```

profile of v0, /device:TPU:0, one launch (start us, length us, event | category | flops | bytes accessed | tf_op | source)
XLA Modules:
  0.0 70.8 jit_solution(4488927391748596661)
XLA Ops:
  0.6 0.0 copy-start
  0.6 0.9 %copy-done = f32[2,4,64,128]{3,2,1,0:T(8,128)S(1)} copy-done((f32[2,4,64,128]{3,2,1,0:T(8,128)S(1)}, f32[2,4,64,128]{3,2,1,0:T(8,128)}, u32[]{:S(2)}) %copy-start) | copy-done | bytes 262168
  1.6 0.0 copy-start.1
  1.6 0.9 %copy-done.1 = s32[4,64,128]{2,1,0:T(8,128)S(1)} copy-done((s32[4,64,128]{2,1,0:T(8,128)S(1)}, s32[4,64,128]{2,1,0:T(8,128)}, u32[]{:S(2)}) %copy-start.1) | copy-done | bytes 131096
  2.5 0.0 copy-start.2
  2.5 0.8 %copy-done.2 = f32[128,128]{1,0:T(8,128)S(1)} copy-done((f32[128,128]{1,0:T(8,128)S(1)}, f32[128,128]{1,0:T(8,128)}, u32[]{:S(2)}) %copy-start.2) | copy-done | bytes 65560
  3.3 0.0 copy-start.3
  3.3 0.8 %copy-done.3 = f32[64,128]{1,0:T(8,128)S(1)} copy-done((f32[64,128]{1,0:T(8,128)S(1)}, f32[64,128]{1,0:T(8,128)}, u32[]{:S(2)}) %copy-start.3) | copy-done | bytes 32792
  4.1 0.0 copy-start.4
  4.1 0.7 copy-done.4
  4.8 64.1 %shard_map.76 = (f32[2,4,64,128]{3,2,1,0:T(8,128)S(1)}, f32[2,4,64,128]{3,2,1,0:T(8,128)S(1)}, f32[2,64]{1,0:T(2,128)S(1)}) custom-call(f32[2,4,64,128]{3,2,1,0:T(8,128)S(1)} %copy-done, s32[4,64,128]{2,1,0:T(8,128)S(1)} %copy-done.1, s32[2,64]{1,0:T(2,128)S(1)} %copy-done.4, f32[128,128]{1,0:T(8,128)S(1)} %copy-done.2, f32[64,128]{1,0:T(8,128)S(1)} %copy-done.3), custom_call_target="tpu_custom_call" | custom-call | tf_op jit(solution)/shard_map/pallas_call | solution.py:600
  68.8 0.7 copy.11
  69.6 0.7 copy.12
  70.3 0.6 copy.13
Async XLA Ops:
  0.6 1.0 %copy-start = (f32[2,4,64,128]{3,2,1,0:T(8,128)S(1)}, f32[2,4,64,128]{3,2,1,0:T(8,128)}, u32[]{:S(2)}) copy-start(f32[2,4,64,128]{3,2,1,0:T(8,128)} %src.1) | copy-start | bytes 786436
  1.6 0.9 %copy-start.1 = (s32[4,64,128]{2,1,0:T(8,128)S(1)}, s32[4,64,128]{2,1,0:T(8,128)}, u32[]{:S(2)}) copy-start(s32[4,64,128]{2,1,0:T(8,128)} %mat.1) | copy-start | bytes 393220
  2.5 0.8 %copy-start.2 = (f32[128,128]{1,0:T(8,128)S(1)}, f32[128,128]{1,0:T(8,128)}, u32[]{:S(2)}) copy-start(f32[128,128]{1,0:T(8,128)} %constant.4.clone.ty) | copy-start | bytes 196612
  3.3 0.8 %copy-start.3 = (f32[64,128]{1,0:T(8,128)S(1)}, f32[64,128]{1,0:T(8,128)}, u32[]{:S(2)}) copy-start(f32[64,128]{1,0:T(8,128)} %constant.5.clone.tx) | copy-start | bytes 98308
  4.1 0.7 copy-start.4
where the time goes:
time: 71.1 us; the launch traced here: 70.8 us
  Pallas kernels  64.1 us (90%)
  local copies, waits for them, and re-layouts  6.09 us (9%)
    pallas_call x1, Pallas kernels, on_device(): pl.pallas_call(functools.partial(kernel, n), out_shape=(jax.ShapeDtypeStr...  64.1 us
    unnamed x13, local copies, waits for them, and re-layouts  6.09 us

commit v1 on v0

--- a/solution.py
+++ b/solution.py
@@ -52,6 +52,25 @@
     lax.fori_loop(lo, hi, step, 0)
 
 
+def planes(lo, hi, group, dst, body):
+    def some(first, count):
+        values = [body(first + j) for j in range(count)]
+        for j, (r, i) in enumerate(values):
+            dst[0, first + j] = r
+            dst[1, first + j] = i
+
+    steps = (hi - lo) // group
+    if steps == 1:
+        some(lo, group)
+    elif steps > 1:
+        loop(0, steps, lambda t: some(lo + t * group, group))
+    if (hi - lo) % group:
+        some(lo + steps * group, (hi - lo) % group)
+
+
+FINE, MIDDLE, COARSE = 2, 4, 6
+
+
 def around(ref, k, p, lane_step):
     x = ref[k, p]
     rows = x.shape[0]
@@ -61,20 +80,20 @@
     return total + (pltpu.roll(x, lane_step, 1) + pltpu.roll(x, lanes - lane_step, 1))
 
 
-def first_sweep(dst, rhs, weight, p):
-    r, i = mul(weight[0, p], weight[1, p], rhs[0, p], rhs[1, p])
-    dst[0, p] = r
-    dst[1, p] = i
-
-
-def sweep(dst, old, rhs, weight, p, lane_step, h2):
-    nr = around(old, 0, p, lane_step)
-    ni = around(old, 1, p, lane_step)
-    if h2 != 1.0:
-        nr, ni = nr * h2, ni * h2
-    r, i = mul(weight[0, p], weight[1, p], rhs[0, p] + nr, rhs[1, p] + ni)
-    dst[0, p] = (1.0 - RELAX) * old[0, p] + r
-    dst[1, p] = (1.0 - RELAX) * old[1, p] + i
+def first_sweep(lo, hi, group, dst, rhs, weight):
+    planes(lo, hi, group, dst, lambda p: mul(weight[0, p], weight[1, p], rhs[0, p], rhs[1, p]))
+
+
+def sweep(lo, hi, group, dst, old, rhs, weight, lane_step, h2):
+    def body(p):
+        nr = around(old, 0, p, lane_step)
+        ni = around(old, 1, p, lane_step)
+        if h2 != 1.0:
+            nr, ni = nr * h2, ni * h2
+        r, i = mul(weight[0, p], weight[1, p], rhs[0, p] + nr, rhs[1, p] + ni)
+        return (1.0 - RELAX) * old[0, p] + r, (1.0 - RELAX) * old[1, p] + i
+
+    planes(lo, hi, group, dst, body)
 
 
 def lane_iota(shape):
@@ -165,14 +184,14 @@
 
 
 def kernel(
-    n, src, mat, ords, ty, tx, sol, res, pup,
-    fx, gx, mx, w0, va, vb, d1, w1, f1, v1a, v1b, w2, f2, v2a, v2b, d2,
+    n, src_in, mat_in, ords_in, ty_in, tx_in, sol, res, pup,
+    ords, ty, tx, in_sem, fx, gx, mx, w0, va, vb, d1, w1, f1, v1a, v1b, w2, f2, v2a, v2b, d2,
     pk1, pk2, tmp, red, spec,
     fine_send, fine_recv, k1_send, k1_recv, k2_send, k2_recv,
     red_send, red_recv, spec_send, spec_recv,
 ):
     me = lax.axis_index("gz")
-    own = src.shape[1]
+    own = mat_in.shape[0]
     depth = own
     half = own // 2
     mid1 = REACH1 * half
@@ -200,24 +219,30 @@
 
     loop(1, n, greet)
 
-    def take(p):
-        m = mat[p]
-        mx[depth + p] = m
-        fx[0, depth + p] = src[0, p]
-        fx[1, depth + p] = src[1, p]
-
-    loop(0, own, take)
+    src = fx.at[:, pl.ds(depth, own)]
+    mat = mx.at[pl.ds(depth, own)]
+    fetches = [
+        pltpu.make_async_copy(a, b, in_sem.at[k])
+        for k, (a, b) in enumerate(
+            ((mat_in, mat), (src_in, src), (ords_in, ords), (ty_in, ty), (tx_in, tx))
+        )
+    ]
+    for fetch in fetches:
+        fetch.start()
+    fetches[0].wait()
 
     for p in range(half):
         a = pick(mat[2 * p], SHIFT_TABLE)
         b = pick(mat[2 * p + 1], SHIFT_TABLE)
         for k in range(2):
-            d1[k, p] = 0.125 * pair_rows(pair_lanes(a[k] + b[k], 1), tmp)
+            d1[k, p] = 0.125 * pair_rows(pair_lanes(a[k] + b[k], 1), tmp.at[2 * p + k])
         pk1[0, REACH1, p] = pack_two(d1[0, p], d1[1, p])
     for k in range(2):
-        d2[k] = 0.125 * pair_rows(pair_lanes(d1[k, 0] + d1[k, 1], 2), tmp)
+        d2[k] = 0.125 * pair_rows(pair_lanes(d1[k, 0] + d1[k, 1], 2), tmp.at[k])
     pk2[0, REACH2] = pack_four(d2[0], d2[1])
 
+    for fetch in fetches[1:]:
+        fetch.wait()
     pl.semaphore_wait(barrier, n - 1)
 
     def send_planes(source, base, target, slot, near, dims):
@@ -241,8 +266,11 @@
         for k in range(1, REACH1 + 1):
             for d in (k, -k):
                 at = which * (2 * REACH1 + 1) + REACH1 - d
+                part = pl.ds(0, half)
+                if k == REACH1:
+                    part = pl.ds(half - 1 if d > 0 else 0, 1)
                 copies[-d] = start(
-                    pk1.at[which, REACH1], pk1.at[which, REACH1 - d],
+                    pk1.at[which, REACH1, part], pk1.at[which, REACH1 - d, part],
                     k1_send.at[at], k1_recv.at[at], d,
                 )
         return copies
@@ -258,12 +286,12 @@
                 )
         return copies
 
-    near_mat = send_planes(mat, 0, mx, 0, True, False)
-    near_src = send_planes(src, 0, fx, 2, True, True)
+    near_mat = send_planes(mx, depth, mx, 0, True, False)
+    near_src = send_planes(fx, depth, fx, 2, True, True)
     shifts1 = send_one(0)
     shifts2 = send_two(0)
-    far_mat = send_planes(mat, 0, mx, 4, False, False)
-    far_src = send_planes(src, 0, fx, 6, False, True)
+    far_mat = send_planes(mx, depth, mx, 4, False, False)
+    far_src = send_planes(fx, depth, fx, 6, False, True)
 
     def inside(plane, count):
         return jnp.where(jnp.logical_and(plane >= 0, plane < count), 1.0, 0.0).astype(F32)
@@ -271,41 +299,30 @@
     def weight0(p):
         m = inside(me * own + p - depth, n * own)
         r, i = pick(mx[p], WEIGHT_TABLE)
-        w0[0, p] = r * m
-        w0[1, p] = i * m
+        return r * m, i * m
 
     def weight1(p):
         r, i = unpack_two(pk1[0, p // half, p % half])
         r, i = invert(r + 1.5, i)
         m = inside(me * half + p - mid1, n * half)
-        w1[0, p] = r * m
-        w1[1, p] = i * m
+        return r * m, i * m
 
     def weight2(p):
         (rt, rb), (it, ib) = unpack_four(pk2[0, p])
-        rows = rt.shape[0]
         m = inside(me + p - REACH2, n)
-        for at, (r, i) in enumerate(((rt, it), (rb, ib))):
-            r, i = invert(r + 0.375, i)
-            w2[0, p, at * rows : (at + 1) * rows] = r * m
-            w2[1, p, at * rows : (at + 1) * rows] = i * m
+        r, i = invert(jnp.concatenate([rt, rb]) + 0.375, jnp.concatenate([it, ib]))
+        return r * m, i * m
 
     def take1(which):
         def body(p):
-            r, i = unpack_two(pk1[which, p // half, p % half])
-            f1[0, p] = r
-            f1[1, p] = i
+            return unpack_two(pk1[which, p // half, p % half])
 
         return body
 
     def take2(which):
         def body(p):
             (rt, rb), (it, ib) = unpack_four(pk2[which, p])
-            rows = rt.shape[0]
-            f2[0, p, 0:rows] = rt
-            f2[0, p, rows : 2 * rows] = rb
-            f2[1, p, 0:rows] = it
-            f2[1, p, rows : 2 * rows] = ib
+            return jnp.concatenate([rt, rb]), jnp.concatenate([it, ib])
 
         return body
 
@@ -314,11 +331,11 @@
         if which == 1:
             for copy in near_mat:
                 copy.wait_recv()
-            loop(begin - 2, end + 2, weight0)
+            planes(begin - 2, end + 2, FINE, w0, weight0)
         for copy in near:
             copy.wait_recv()
-        loop(begin - 2, end + 2, lambda p: first_sweep(va, f, w0, p))
-        loop(begin - 1, end + 1, lambda p: sweep(vb, va, f, w0, p, 1, 1.0))
+        first_sweep(begin - 2, end + 2, FINE, va, f, w0)
+        sweep(begin - 1, end + 1, FINE, vb, va, f, w0, 1, 1.0)
 
         def down(q):
             total = [None, None]
@@ -329,7 +346,9 @@
                 for k, d in enumerate((dr, di)):
                     e = (f[k, p] - d) + around(vb, k, p, 1)
                     total[k] = e if s == 0 else total[k] + e
-            parts = [0.125 * pair_rows(pair_lanes(t, 1), tmp) for t in total]
+            parts = [
+                0.125 * pair_rows(pair_lanes(t, 1), tmp.at[2 * q + k]) for k, t in enumerate(total)
+            ]
             f1[0, mid1 + q] = parts[0]
             f1[1, mid1 + q] = parts[1]
             pk1[which, REACH1, q] = pack_two(parts[0], parts[1])
@@ -341,14 +360,14 @@
         if which == 1:
             for d in (-1, 1):
                 shifts1[d].wait_recv()
-            loop(mid1 - half, mid1 + 2 * half, weight1)
+            planes(mid1 - half, mid1 + 2 * half, MIDDLE, w1, weight1)
 
         for d in (-1, 1):
             ones[d].wait_recv()
-        loop(mid1 - half, mid1, take1(which))
-        loop(mid1 + half, mid1 + 2 * half, take1(which))
-        loop(mid1 - 2, mid1 + half + 2, lambda p: first_sweep(v1a, f1, w1, p))
-        loop(mid1 - 1, mid1 + half + 1, lambda p: sweep(v1b, v1a, f1, w1, p, 2, 0.25))
+        planes(mid1 - half, mid1, MIDDLE, f1, take1(which))
+        planes(mid1 + half, mid1 + 2 * half, MIDDLE, f1, take1(which))
+        first_sweep(mid1 - 2, mid1 + half + 2, MIDDLE, v1a, f1, w1)
+        sweep(mid1 - 1, mid1 + half + 1, MIDDLE, v1b, v1a, f1, w1, 2, 0.25)
 
         parts = []
         total = [None, None]
@@ -358,71 +377,73 @@
             for k, d in enumerate((dr, di)):
                 e = (f1[k, p] - d) + 0.25 * around(v1b, k, p, 2)
                 total[k] = e if q == 0 else total[k] + e
-        parts = [0.125 * pair_rows(pair_lanes(t, 2), tmp) for t in total]
+        parts = [0.125 * pair_rows(pair_lanes(t, 2), tmp.at[k]) for k, t in enumerate(total)]
         pk2[which, REACH2] = pack_four(parts[0], parts[1])
         twos = send_two(which)
 
         if which == 1:
             for copy in far_mat:
                 copy.wait_recv()
-            loop(0, begin - 2, weight0)
-            loop(end + 2, end + depth, weight0)
+            planes(0, begin - 2, FINE, w0, weight0)
+            planes(end + 2, end + depth, FINE, w0, weight0)
             for d in range(2, REACH1 + 1):
                 shifts1[d].wait_recv()
                 shifts1[-d].wait_recv()
-            loop(1, mid1 - half, weight1)
-            loop(mid1 + 2 * half, 2 * mid1 + half - 1, weight1)
+            planes(1, mid1 - half, MIDDLE, w1, weight1)
+            planes(mid1 + 2 * half, 2 * mid1 + half - 1, MIDDLE, w1, weight1)
         for d in range(2, REACH1 + 1):
             ones[d].wait_recv()
             ones[-d].wait_recv()
-        loop(1, mid1 - half, take1(which))
-        loop(mid1 + 2 * half, 2 * mid1 + half - 1, take1(which))
-        loop(1, mid1 - 2, lambda p: first_sweep(v1a, f1, w1, p))
-        loop(mid1 + half + 2, 2 * mid1 + half - 1, lambda p: first_sweep(v1a, f1, w1, p))
-        loop(2, mid1 - 1, lambda p: sweep(v1b, v1a, f1, w1, p, 2, 0.25))
-        loop(mid1 + half + 1, 2 * mid1 + half - 2, lambda p: sweep(v1b, v1a, f1, w1, p, 2, 0.25))
+        planes(1, mid1 - half, MIDDLE, f1, take1(which))
+        planes(mid1 + 2 * half, 2 * mid1 + half - 1, MIDDLE, f1, take1(which))
+        first_sweep(1, mid1 - 2, MIDDLE, v1a, f1, w1)
+        first_sweep(mid1 + half + 2, 2 * mid1 + half - 1, MIDDLE, v1a, f1, w1)
+        sweep(2, mid1 - 1, MIDDLE, v1b, v1a, f1, w1, 2, 0.25)
+        sweep(mid1 + half + 1, 2 * mid1 + half - 2, MIDDLE, v1b, v1a, f1, w1, 2, 0.25)
         for copy in far:
             copy.wait_recv()
-        loop(0, begin - 2, lambda p: first_sweep(va, f, w0, p))
-        loop(end + 2, end + depth, lambda p: first_sweep(va, f, w0, p))
-        loop(1, begin - 1, lambda p: sweep(vb, va, f, w0, p, 1, 1.0))
-        loop(end + 1, end + depth - 1, lambda p: sweep(vb, va, f, w0, p, 1, 1.0))
+        first_sweep(0, begin - 2, FINE, va, f, w0)
+        first_sweep(end + 2, end + depth, FINE, va, f, w0)
+        sweep(1, begin - 1, FINE, vb, va, f, w0, 1, 1.0)
+        sweep(end + 1, end + depth - 1, FINE, vb, va, f, w0, 1, 1.0)
         if which == 1:
             for d in range(1, REACH2 + 1):
                 shifts2[d].wait_recv()
                 shifts2[-d].wait_recv()
-            loop(0, 2 * REACH2 + 1, weight2)
+            planes(0, 2 * REACH2 + 1, COARSE, w2, weight2)
 
         for d in range(1, REACH2 + 1):
             twos[d].wait_recv()
             twos[-d].wait_recv()
-        loop(0, 2 * REACH2 + 1, take2(which))
-        loop(0, 2 * REACH2 + 1, lambda p: first_sweep(v2a, f2, w2, p))
-        loop(1, 2 * REACH2, lambda p: sweep(v2b, v2a, f2, w2, p, 4, 0.0625))
-        loop(2, 2 * REACH2 - 1, lambda p: sweep(v2a, v2b, f2, w2, p, 4, 0.0625))
-        loop(3, 2 * REACH2 - 2, lambda p: sweep(v2b, v2a, f2, w2, p, 4, 0.0625))
+        planes(0, 2 * REACH2 + 1, COARSE, f2, take2(which))
+        first_sweep(0, 2 * REACH2 + 1, COARSE, v2a, f2, w2)
+        sweep(1, 2 * REACH2, COARSE, v2b, v2a, f2, w2, 4, 0.0625)
+        sweep(2, 2 * REACH2 - 1, COARSE, v2a, v2b, f2, w2, 4, 0.0625)
+        sweep(3, 2 * REACH2 - 2, COARSE, v2b, v2a, f2, w2, 4, 0.0625)
 
         def raise1(c):
             p = (c - REACH2 + REACH1) * half
             for k in range(2):
-                x = spread_rows(v2b[k, c], tmp)
+                x = spread_rows(v2b[k, c], tmp.at[2 * (c % 2) + k])
                 v1b[k, p] = v1b[k, p] + x
                 v1b[k, p + 1] = v1b[k, p + 1] + x
 
-        loop(REACH2 - 2, REACH2 + 3, raise1)
-        loop(mid1 - 3, mid1 + half + 3, lambda p: sweep(v1a, v1b, f1, w1, p, 2, 0.25))
-        loop(mid1 - 2, mid1 + half + 2, lambda p: sweep(v1b, v1a, f1, w1, p, 2, 0.25))
+        for c in range(REACH2 - 2, REACH2 + 3):
+            raise1(c)
+        sweep(mid1 - 3, mid1 + half + 3, MIDDLE, v1a, v1b, f1, w1, 2, 0.25)
+        sweep(mid1 - 2, mid1 + half + 2, MIDDLE, v1b, v1a, f1, w1, 2, 0.25)
 
         def raise0(c):
             p = depth + 2 * (c - mid1)
             for k in range(2):
-                x = spread_rows(v1b[k, c], tmp)
+                x = spread_rows(v1b[k, c], tmp.at[2 * (c % 2) + k])
                 vb[k, p] = vb[k, p] + x
                 vb[k, p + 1] = vb[k, p + 1] + x
 
-        loop(mid1 - 2, mid1 + half + 2, raise0)
-        loop(begin - 2, end + 2, lambda p: sweep(va, vb, f, w0, p, 1, 1.0))
-        loop(begin - 1, end + 1, lambda p: sweep(vb, va, f, w0, p, 1, 1.0))
+        for c in range(mid1 - 2, mid1 + half + 2):
+            raise0(c)
+        sweep(begin - 2, end + 2, FINE, va, vb, f, w0, 1, 1.0)
+        sweep(begin - 1, end + 1, FINE, vb, va, f, w0, 1, 1.0)
 
     def image_of(p):
         c = pick(mx[p], IMAGE_TABLE)
@@ -512,7 +533,7 @@
 
     cycle(1, fx, near_src, far_src)
 
-    zero = jnp.zeros((8, src.shape[3]), F32)
+    zero = jnp.zeros((8, fx.shape[3]), F32)
     sums = [zero, zero, zero]
     for p in range(own):
         r, i = image_of(depth + p)
@@ -604,15 +625,16 @@
             jax.ShapeDtypeStruct(source_term.shape, F32),
             jax.ShapeDtypeStruct(orders.shape, F32),
         ),
-        in_specs=[whole] * 5,
+        in_specs=[pl.BlockSpec(memory_space=pl.ANY)] * 5,
         out_specs=(whole,) * 3,
         scratch_shapes=[
+            vm(orders.shape, jnp.int32), vm(ty.shape, F32), vm(tx.shape, F32), dma((5,)),
             fine, fine, vm((3 * own, nx, ny), jnp.int32), fine, fine, fine,
             vm((2, half, nx // 2, ny), F32), one, one, one, one,
             two, two, two, two, vm((2, nx // 4, ny), F32),
             vm((3, 2 * REACH1 + 1, half, nx // 2, ny), F32),
             vm((3, planes2, nx // 8, ny), F32),
-            vm((nx, ny), F32),
+            vm((2 * half, nx, ny), F32),
             vm((2, n, 8, ny), F32),
             vm((2, HARM, 2 * HALF), F32),
             dma((12,)), dma((12,)), dma((ext1,)), dma((ext1,)), dma((ext2,)), dma((ext2,)),

time: 71.1 us -> 58.9 us (0.83)
  Pallas kernels: 64.1 us -> 51.9 us
    pallas_call x1, Pallas kernels: 64.1 us -> 51.9 us  [on_device(): pl.pallas_call(functools.partial(kernel, n), out_shape=(jax.ShapeDtypeStr...]
where the time goes in v1:
time: 58.9 us; the launch traced here: 58.6 us
  Pallas kernels  51.9 us (88%)
  local copies, waits for them, and re-layouts  6.09 us (10%)
  between operations  0.65 us (1%)
    pallas_call x1, Pallas kernels, on_device(): pl.pallas_call(functools.partial(kernel, n), out_shape=(jax.ShapeDtypeStr...  51.9 us
    unnamed x13, local copies, waits for them, and re-layouts  6.09 us

profile of v1, /device:TPU:0, one launch (start us, length us, event | category | flops | bytes accessed | tf_op | source)
XLA Modules:
  0.0 58.6 jit_solution(14607929532675636391)
XLA Ops:
  0.6 0.0 copy-start
  0.6 0.9 %copy-done = f32[2,4,64,128]{3,2,1,0:T(8,128)S(1)} copy-done((f32[2,4,64,128]{3,2,1,0:T(8,128)S(1)}, f32[2,4,64,128]{3,2,1,0:T(8,128)}, u32[]{:S(2)}) %copy-start) | copy-done | bytes 262168
  1.6 0.0 copy-start.1
  1.6 0.9 %copy-done.1 = s32[4,64,128]{2,1,0:T(8,128)S(1)} copy-done((s32[4,64,128]{2,1,0:T(8,128)S(1)}, s32[4,64,128]{2,1,0:T(8,128)}, u32[]{:S(2)}) %copy-start.1) | copy-done | bytes 131096
  2.5 0.0 copy-start.2
  2.5 0.8 %copy-done.2 = f32[128,128]{1,0:T(8,128)S(1)} copy-done((f32[128,128]{1,0:T(8,128)S(1)}, f32[128,128]{1,0:T(8,128)}, u32[]{:S(2)}) %copy-start.2) | copy-done | bytes 65560
  3.3 0.0 copy-start.3
  3.3 0.8 %copy-done.3 = f32[64,128]{1,0:T(8,128)S(1)} copy-done((f32[64,128]{1,0:T(8,128)S(1)}, f32[64,128]{1,0:T(8,128)}, u32[]{:S(2)}) %copy-start.3) | copy-done | bytes 32792
  4.1 0.0 copy-start.4
  4.1 0.7 %copy-done.4 = s32[2,64]{1,0:T(2,128)S(1)} copy-done((s32[2,64]{1,0:T(2,128)S(1)}, s32[2,64]{1,0:T(2,128)}, u32[]{:S(2)}) %copy-start.4) | copy-done | bytes 536
  4.8 51.9 %shard_map.76 = (f32[2,4,64,128]{3,2,1,0:T(8,128)S(1)}, f32[2,4,64,128]{3,2,1,0:T(8,128)S(1)}, f32[2,64]{1,0:T(2,128)S(1)}) custom-call(f32[2,4,64,128]{3,2,1,0:T(8,128)S(1)} %copy-done, s32[4,64,128]{2,1,0:T(8,128)S(1)} %copy-done.1, s32[2,64]{1,0:T(2,128)S(1)} %copy-done.4, f32[128,128]{1,0:T(8,128)S(1)} %copy-done.2, f32[64,128]{1,0:T(8,128)S(1)} %copy-done.3), custom_call_target="tpu_custom_call" | custom-call | tf_op jit(solution)/shard_map/pallas_call | solution.py:621
  56.7 0.7 %copy.11 = f32[2,4,64,128]{3,2,1,0:T(8,128)} copy(f32[2,4,64,128]{3,2,1,0:T(8,128)S(1)} %get-tuple-element.6) | data formatting | bytes 524288
  57.4 0.7 %copy.12 = f32[2,4,64,128]{3,2,1,0:T(8,128)} copy(f32[2,4,64,128]{3,2,1,0:T(8,128)S(1)} %get-tuple-element.7) | data formatting | bytes 524288
  58.1 0.6 copy.13
Async XLA Ops:
  0.6 1.0 %copy-start = (f32[2,4,64,128]{3,2,1,0:T(8,128)S(1)}, f32[2,4,64,128]{3,2,1,0:T(8,128)}, u32[]{:S(2)}) copy-start(f32[2,4,64,128]{3,2,1,0:T(8,128)} %src_in.1) | copy-start | bytes 786436
  1.6 0.9 %copy-start.1 = (s32[4,64,128]{2,1,0:T(8,128)S(1)}, s32[4,64,128]{2,1,0:T(8,128)}, u32[]{:S(2)}) copy-start(s32[4,64,128]{2,1,0:T(8,128)} %mat_in.1) | copy-start | bytes 393220
  2.5 0.8 %copy-start.2 = (f32[128,128]{1,0:T(8,128)S(1)}, f32[128,128]{1,0:T(8,128)}, u32[]{:S(2)}) copy-start(f32[128,128]{1,0:T(8,128)} %constant.4.clone.ty_in) | copy-start | bytes 196612
  3.3 0.8 %copy-start.3 = (f32[64,128]{1,0:T(8,128)S(1)}, f32[64,128]{1,0:T(8,128)}, u32[]{:S(2)}) copy-start(f32[64,128]{1,0:T(8,128)} %constant.5.clone.tx_in) | copy-start | bytes 98308
  4.1 0.7 %copy-start.4 = (s32[2,64]{1,0:T(2,128)S(1)}, s32[2,64]{1,0:T(2,128)}, u32[]{:S(2)}) copy-start(s32[2,64]{1,0:T(2,128)} %ords_in.1) | copy-start | bytes 1540
